TPU v7x, 512 devices: a whole 4x8x8 slice. The times are simulated.
512 devices in a mesh: seq: 64 (over z_hi, y, core), head: 8 (over x, z_lo).
Axes of the slice: x: 4, y: 8, z: 8 (z_hi: 4, z_lo: 2; z = z_hi * 2 + z_lo), core: 2. Of those that a mesh axis runs over, the one named last changes fastest.
Arguments:
- query_rows: bfloat16 [32768, 8192], P('seq', 'head'), may hold values from -12 to 12
- key_rows: bfloat16 [32768, 1024], P(('seq', 'head')), may hold values from -6 to 6
- value_rows: bfloat16 [32768, 1024], P(('seq', 'head')), may hold values from -6 to 6
- tree_mask: int32 [64, 5], P('seq'), may hold values from 0 to 1, as said below
- token_depth: int32 [32768], P('seq'), may hold values from 0 to 7
Outputs:
- attended: bfloat16 [32768, 8192], P('seq', 'head')
- log_sums: float32 [64, 32768], P('head', 'seq')
Inputs may be any that keep to these rules, and one draw needn't show every extreme that they name: `tree_mask`: column 0 of every row is 1; entry (i, s) is 0 where i < s.
All inputs are finite; a program needn't handle non-finite values.
Results may differ from a plain program's by a relative error of at most 0.0031.
Values may be sent and summed in bfloat16 or wider, within the bound.
A program may use at most 64 MiB of HBM per device.

v0:
```python
import jax
import jax.numpy as jnp
from jax import lax
from jax.sharding import PartitionSpec as P

HD = 128
REACH = 4


def passed_along(value, axis, steps):
    count = lax.axis_size(axis)
    initial, last = (max(0, -steps), min(count, count - steps))
    return lax.ppermute(value, axis, [(source, source + steps) for source in range(initial, last)])


def body(query_rows, key_rows, value_rows, tree_mask, token_depth):
    key_local, value_local = (
        lax.all_to_all(key_rows, "head", split_axis=1, concat_axis=0, tiled=True),
        lax.all_to_all(value_rows, "head", split_axis=1, concat_axis=0, tiled=True),
    )
    bundle = (key_local, value_local, token_depth)
    gathered = [bundle]
    current = bundle
    for offset in range(REACH):
        current = passed_along((current[0], current[1], current[2]), "seq", 1)
        gathered.append(current)
    block_len = query_rows.shape[0]
    key_cat = jnp.concatenate([member[0] for member in gathered], 0)
    value_cat = jnp.concatenate([member[1] for member in gathered], 0)
    depth_cat = jnp.concatenate([member[2] for member in gathered], 0)
    key_count = (REACH + 1) * block_len
    key_slot = jnp.arange(key_count) // block_len
    key_place = jnp.arange(key_count) % block_len
    mask_line = tree_mask[0]
    picked = (
        jnp.sum(
            jnp.where(key_slot[:, None] == jnp.arange(REACH + 1)[None, :], mask_line[None, :], 0), 1
        )
        > 0
    )
    position = jnp.arange(block_len)
    visible = picked[None, :] & jnp.where(
        key_slot[None, :] == 0,
        key_place[None, :] <= position[:, None],
        depth_cat[None, :] <= token_depth[:, None],
    )
    local_heads = query_rows.shape[1] // HD
    score_scale = HD ** (-0.5)

    def one_head(head_index):
        query_head = lax.dynamic_slice_in_dim(query_rows, head_index * HD, HD, 1)
        scores = (
            lax.dot_general(
                query_head, key_cat, (((1,), (1,)), ((), ())), preferred_element_type=jnp.float32
            )
            * score_scale
        )
        masked = jnp.where(visible, scores, -jnp.inf)
        row_top = jnp.max(masked, 1)
        exp_terms = jnp.exp(masked - row_top[:, None])
        row_total = jnp.sum(exp_terms, 1)
        weights = exp_terms.astype(jnp.bfloat16)
        mixed_rows = (
            jnp.dot(weights, value_cat, preferred_element_type=jnp.float32) / row_total[:, None]
        )
        return (mixed_rows.astype(jnp.bfloat16), row_top + jnp.log(row_total))

    mixed_all, log_sums = lax.map(one_head, jnp.arange(local_heads, dtype=jnp.int32))
    attended = jnp.transpose(mixed_all, (1, 0, 2)).reshape(block_len, local_heads * HD)
    return (attended, log_sums)


def solution(mesh):
    return jax.shard_map(
        body,
        mesh=mesh,
        in_specs=(
            P("seq", "head"),
            P(("seq", "head"), None),
            P(("seq", "head"), None),
            P("seq", None),
            P("seq"),
        ),
        out_specs=(P("seq", "head"), P("head", "seq")),
        check_vma=False,
    )
```

profile of v0, /device:TPU:256, one launch (start us, length us, event | category | flops | bytes accessed | tf_op | source)
XLA Modules:
  0.0 194.3 jit_solution(11857590434213144785)
XLA Ops:
  2.2 5.2 %all-to-all-start.1 = ((bf16[64,8,128]{2,0,1:T(8,128)(2,1)}), bf16[64,8,128]{2,0,1:T(8,128)(2,1)S(1)}, u32[]{:S(2)}, u32[]{:S(2)}) async-start(bf16[64,8,128]{2,0,1:T(8,128)(2,1)} %copy_bitcast_fusion.1), calls=%async_computation.1 | async-start | bytes 262144 | tf_op jit(solution)/shard_map/all_to_all | solution.py:19
  12.4 4.3 %collective-permute-done.4 = s32[512]{0:T(512)S(1)} collective-permute-done((s32[512]{0:T(512)}, s32[512]{0:T(512)S(1)}, u32[]{:S(2)}, u32[]{:S(2)}) %collective-permute-start.4) | collective-permute-done | bytes 2080 | tf_op jit(solution)/shard_map/ppermute | solution.py:13
  18.7 7.2 %collective-permute-done.5 = s32[512]{0:T(512)S(1)} collective-permute-done((s32[512]{0:T(512)S(1)}, s32[512]{0:T(512)S(1)}, u32[]{:S(2)}, u32[]{:S(2)}) %collective-permute-start.5) | collective-permute-done | bytes 2080 | tf_op jit(solution)/shard_map/ppermute | solution.py:13
  27.8 7.3 %collective-permute-done.6 = s32[512]{0:T(512)S(1)} collective-permute-done((s32[512]{0:T(512)S(1)}, s32[512]{0:T(512)S(1)}, u32[]{:S(2)}, u32[]{:S(2)}) %collective-permute-start.6) | collective-permute-done | bytes 2080 | tf_op jit(solution)/shard_map/ppermute | solution.py:13
  37.0 5.7 %all-to-all-start = ((bf16[64,8,128]{2,0,1:T(8,128)(2,1)}), bf16[64,8,128]{2,0,1:T(8,128)(2,1)S(1)}, u32[]{:S(2)}, u32[]{:S(2)}) async-start(bf16[64,8,128]{2,0,1:T(8,128)(2,1)} %copy_bitcast_fusion.2), calls=%async_computation | async-start | bytes 262144 | tf_op jit(solution)/shard_map/all_to_all | solution.py:18
  46.1 3.2 %all-to-all-done = bf16[64,8,128]{2,0,1:T(8,128)(2,1)S(1)} async-done(((bf16[64,8,128]{2,0,1:T(8,128)(2,1)}), bf16[64,8,128]{2,0,1:T(8,128)(2,1)S(1)}, u32[]{:S(2)}, u32[]{:S(2)}) %all-to-all-start) | async-done | bytes 131104 | tf_op jit(solution)/shard_map/all_to_all | solution.py:18
  51.3 4.8 %collective-permute-done.8 = bf16[512,128]{1,0:T(8,128)(2,1)S(1)} collective-permute-done((bf16[512,128]{1,0:T(8,128)(2,1)S(1)}, bf16[512,128]{1,0:T(8,128)(2,1)S(1)}, u32[]{:S(2)}, u32[]{:S(2)}) %collective-permute-start.8) | collective-permute-done | bytes 131104 | tf_op jit(solution)/shard_map/ppermute | solution.py:13
  58.0 2.5 %collective-permute-done = bf16[512,128]{1,0:T(8,128)(2,1)S(1)} collective-permute-done((bf16[512,128]{1,0:T(8,128)(2,1)S(1)}, bf16[512,128]{1,0:T(8,128)(2,1)S(1)}, u32[]{:S(2)}, u32[]{:S(2)}) %collective-permute-start) | collective-permute-done | bytes 131104 | tf_op jit(solution)/shard_map/ppermute | solution.py:13
  62.5 5.1 %collective-permute-done.9 = bf16[512,128]{1,0:T(8,128)(2,1)S(1)} collective-permute-done((bf16[512,128]{1,0:T(8,128)(2,1)S(1)}, bf16[512,128]{1,0:T(8,128)(2,1)S(1)}, u32[]{:S(2)}, u32[]{:S(2)}) %collective-permute-start.9) | collective-permute-done | bytes 131104 | tf_op jit(solution)/shard_map/ppermute | solution.py:13
  69.5 2.5 %collective-permute-done.1 = bf16[512,128]{1,0:T(8,128)(2,1)S(1)} collective-permute-done((bf16[512,128]{1,0:T(8,128)(2,1)S(1)}, bf16[512,128]{1,0:T(8,128)(2,1)S(1)}, u32[]{:S(2)}, u32[]{:S(2)}) %collective-permute-start.1) | collective-permute-done | bytes 131104 | tf_op jit(solution)/shard_map/ppermute | solution.py:13
  73.9 5.3 %collective-permute-done.10 = bf16[512,128]{1,0:T(8,128)(2,1)S(1)} collective-permute-done((bf16[512,128]{1,0:T(8,128)(2,1)S(1)}, bf16[512,128]{1,0:T(8,128)(2,1)S(1)}, u32[]{:S(2)}, u32[]{:S(2)}) %collective-permute-start.10) | collective-permute-done | bytes 131104 | tf_op jit(solution)/shard_map/ppermute | solution.py:13
  85.4 5.6 %collective-permute-done.11 = bf16[512,128]{1,0:T(8,128)(2,1)S(1)} collective-permute-done((bf16[512,128]{1,0:T(8,128)(2,1)S(1)}, bf16[512,128]{1,0:T(8,128)(2,1)S(1)}, u32[]{:S(2)}, u32[]{:S(2)}) %collective-permute-start.11) | collective-permute-done | bytes 131104 | tf_op jit(solution)/shard_map/ppermute | solution.py:13
  91.0 3.9 %collective-permute-done.3 = bf16[512,128]{1,0:T(8,128)(2,1)S(1)} collective-permute-done((bf16[512,128]{1,0:T(8,128)(2,1)S(1)}, bf16[512,128]{1,0:T(8,128)(2,1)S(1)}, u32[]{:S(2)}, u32[]{:S(2)}) %collective-permute-start.3) | collective-permute-done | bytes 131104 | tf_op jit(solution)/shard_map/ppermute | solution.py:13
  94.9 98.3 %while.13 = (s32[]{:T(128)}, bf16[8,512,128]{2,1,0:T(8,128)(2,1)S(1)}, f32[8,512]{1,0:T(8,128)}, s32[8]{0:T(128)S(1)}, bf16[512,1024]{1,0:T(8,128)(2,1)}, /*inde...) while((s32[]{:T(128)}, ...), condition=%wide.region_4.5_spmd.clone, body=%wide.region_1.4_spmd.clone.sunk | while | flops 685637120 | bytes 38321396 | solution.py:68
  96.1 3.1 %fusion.45 = (f32[512]{0:T(512)S(1)}, f32[512,2560]{1,0:T(8,128)S(1)}) fusion(bf16[2560,128]{1,0:T(8,128)(2,1)S(1)} %get-tuple-element.220, bf16[512,1024]{1,0:T(8,128)(2,1)} %get-tuple-element.219, s32[]{:T(128)S(6)} %select_n.63, s32[512]{0:T(512)} %get-tuple-element.223, s32[2560]{0:T(1024)S(1)} %get-tuple-element.224, ...), kind=kOutput, calls=%fused_computation.50.clone.1 | convolution fusion | flops 344718848 | bytes 6059012 | tf_op jit(solution)/shard_map/while/body/eval_jaxpr/dot_general | solution.py:53
  103.7 3.5 %fusion.47 = bf16[8,512,128]{2,1,0:T(8,128)(2,1)S(1)} fusion(bf16[8,512,128]{2,1,0:T(8,128)(2,1)S(1)} %get-tuple-element.200, s32[]{:T(128)} %get-tuple-element.199, bf16[2560,128]{1,0:T(8,128)(2,1)S(1)} %get-tuple-element.221, f32[512,2560]{1,0:T(8,128)} %copy-done.1, f32[512]{0:T(512)S(1)} %get-tuple-element.182, f32[512]{0:T(512)S(1)} %fusion.46), kind=kOutput, calls=%fused_computation.13.clone.1 | convolution fusion | flops 338296832 | bytes 6033412 | tf_op jit(solution)/shard_map/while/body/eval_jaxpr/dot_general | solution.py:64
  108.4 3.1 %fusion.45 = (f32[512]{0:T(512)S(1)}, f32[512,2560]{1,0:T(8,128)S(1)}) fusion(bf16[2560,128]{1,0:T(8,128)(2,1)S(1)} %get-tuple-element.220, bf16[512,1024]{1,0:T(8,128)(2,1)} %get-tuple-element.219, s32[]{:T(128)S(6)} %select_n.63, s32[512]{0:T(512)} %get-tuple-element.223, s32[2560]{0:T(1024)S(1)} %get-tuple-element.224, ...), kind=kOutput, calls=%fused_computation.50.clone.1 | convolution fusion | flops 344718848 | bytes 6059012 | tf_op jit(solution)/shard_map/while/body/eval_jaxpr/dot_general | solution.py:53
  111.5 2.3 %copy-done.1 = f32[512,2560]{1,0:T(8,128)} copy-done((f32[512,2560]{1,0:T(8,128)}, f32[512,2560]{1,0:T(8,128)S(1)}, u32[]{:S(2)}) %copy-start.1) | copy-done | bytes 5242904 | tf_op jit(solution)/shard_map/while
  116.0 3.5 %fusion.47 = bf16[8,512,128]{2,1,0:T(8,128)(2,1)S(1)} fusion(bf16[8,512,128]{2,1,0:T(8,128)(2,1)S(1)} %get-tuple-element.200, s32[]{:T(128)} %get-tuple-element.199, bf16[2560,128]{1,0:T(8,128)(2,1)S(1)} %get-tuple-element.221, f32[512,2560]{1,0:T(8,128)} %copy-done.1, f32[512]{0:T(512)S(1)} %get-tuple-element.182, f32[512]{0:T(512)S(1)} %fusion.46), kind=kOutput, calls=%fused_computation.13.clone.1 | convolution fusion | flops 338296832 | bytes 6033412 | tf_op jit(solution)/shard_map/while/body/eval_jaxpr/dot_general | solution.py:64
  120.7 3.1 %fusion.45 = (f32[512]{0:T(512)S(1)}, f32[512,2560]{1,0:T(8,128)S(1)}) fusion(bf16[2560,128]{1,0:T(8,128)(2,1)S(1)} %get-tuple-element.220, bf16[512,1024]{1,0:T(8,128)(2,1)} %get-tuple-element.219, s32[]{:T(128)S(6)} %select_n.63, s32[512]{0:T(512)} %get-tuple-element.223, s32[2560]{0:T(1024)S(1)} %get-tuple-element.224, ...), kind=kOutput, calls=%fused_computation.50.clone.1 | convolution fusion | flops 344718848 | bytes 6059012 | tf_op jit(solution)/shard_map/while/body/eval_jaxpr/dot_general | solution.py:53
  128.3 3.5 %fusion.47 = bf16[8,512,128]{2,1,0:T(8,128)(2,1)S(1)} fusion(bf16[8,512,128]{2,1,0:T(8,128)(2,1)S(1)} %get-tuple-element.200, s32[]{:T(128)} %get-tuple-element.199, bf16[2560,128]{1,0:T(8,128)(2,1)S(1)} %get-tuple-element.221, f32[512,2560]{1,0:T(8,128)} %copy-done.1, f32[512]{0:T(512)S(1)} %get-tuple-element.182, f32[512]{0:T(512)S(1)} %fusion.46), kind=kOutput, calls=%fused_computation.13.clone.1 | convolution fusion | flops 338296832 | bytes 6033412 | tf_op jit(solution)/shard_map/while/body/eval_jaxpr/dot_general | solution.py:64
  133.0 3.1 %fusion.45 = (f32[512]{0:T(512)S(1)}, f32[512,2560]{1,0:T(8,128)S(1)}) fusion(bf16[2560,128]{1,0:T(8,128)(2,1)S(1)} %get-tuple-element.220, bf16[512,1024]{1,0:T(8,128)(2,1)} %get-tuple-element.219, s32[]{:T(128)S(6)} %select_n.63, s32[512]{0:T(512)} %get-tuple-element.223, s32[2560]{0:T(1024)S(1)} %get-tuple-element.224, ...), kind=kOutput, calls=%fused_computation.50.clone.1 | convolution fusion | flops 344718848 | bytes 6059012 | tf_op jit(solution)/shard_map/while/body/eval_jaxpr/dot_general | solution.py:53
  140.6 3.5 %fusion.47 = bf16[8,512,128]{2,1,0:T(8,128)(2,1)S(1)} fusion(bf16[8,512,128]{2,1,0:T(8,128)(2,1)S(1)} %get-tuple-element.200, s32[]{:T(128)} %get-tuple-element.199, bf16[2560,128]{1,0:T(8,128)(2,1)S(1)} %get-tuple-element.221, f32[512,2560]{1,0:T(8,128)} %copy-done.1, f32[512]{0:T(512)S(1)} %get-tuple-element.182, f32[512]{0:T(512)S(1)} %fusion.46), kind=kOutput, calls=%fused_computation.13.clone.1 | convolution fusion | flops 338296832 | bytes 6033412 | tf_op jit(solution)/shard_map/while/body/eval_jaxpr/dot_general | solution.py:64
  145.3 3.1 %fusion.45 = (f32[512]{0:T(512)S(1)}, f32[512,2560]{1,0:T(8,128)S(1)}) fusion(bf16[2560,128]{1,0:T(8,128)(2,1)S(1)} %get-tuple-element.220, bf16[512,1024]{1,0:T(8,128)(2,1)} %get-tuple-element.219, s32[]{:T(128)S(6)} %select_n.63, s32[512]{0:T(512)} %get-tuple-element.223, s32[2560]{0:T(1024)S(1)} %get-tuple-element.224, ...), kind=kOutput, calls=%fused_computation.50.clone.1 | convolution fusion | flops 344718848 | bytes 6059012 | tf_op jit(solution)/shard_map/while/body/eval_jaxpr/dot_general | solution.py:53
  152.9 3.5 %fusion.47 = bf16[8,512,128]{2,1,0:T(8,128)(2,1)S(1)} fusion(bf16[8,512,128]{2,1,0:T(8,128)(2,1)S(1)} %get-tuple-element.200, s32[]{:T(128)} %get-tuple-element.199, bf16[2560,128]{1,0:T(8,128)(2,1)S(1)} %get-tuple-element.221, f32[512,2560]{1,0:T(8,128)} %copy-done.1, f32[512]{0:T(512)S(1)} %get-tuple-element.182, f32[512]{0:T(512)S(1)} %fusion.46), kind=kOutput, calls=%fused_computation.13.clone.1 | convolution fusion | flops 338296832 | bytes 6033412 | tf_op jit(solution)/shard_map/while/body/eval_jaxpr/dot_general | solution.py:64
  157.6 3.1 %fusion.45 = (f32[512]{0:T(512)S(1)}, f32[512,2560]{1,0:T(8,128)S(1)}) fusion(bf16[2560,128]{1,0:T(8,128)(2,1)S(1)} %get-tuple-element.220, bf16[512,1024]{1,0:T(8,128)(2,1)} %get-tuple-element.219, s32[]{:T(128)S(6)} %select_n.63, s32[512]{0:T(512)} %get-tuple-element.223, s32[2560]{0:T(1024)S(1)} %get-tuple-element.224, ...), kind=kOutput, calls=%fused_computation.50.clone.1 | convolution fusion | flops 344718848 | bytes 6059012 | tf_op jit(solution)/shard_map/while/body/eval_jaxpr/dot_general | solution.py:53
  165.1 3.5 %fusion.47 = bf16[8,512,128]{2,1,0:T(8,128)(2,1)S(1)} fusion(bf16[8,512,128]{2,1,0:T(8,128)(2,1)S(1)} %get-tuple-element.200, s32[]{:T(128)} %get-tuple-element.199, bf16[2560,128]{1,0:T(8,128)(2,1)S(1)} %get-tuple-element.221, f32[512,2560]{1,0:T(8,128)} %copy-done.1, f32[512]{0:T(512)S(1)} %get-tuple-element.182, f32[512]{0:T(512)S(1)} %fusion.46), kind=kOutput, calls=%fused_computation.13.clone.1 | convolution fusion | flops 338296832 | bytes 6033412 | tf_op jit(solution)/shard_map/while/body/eval_jaxpr/dot_general | solution.py:64
  169.9 3.1 %fusion.45 = (f32[512]{0:T(512)S(1)}, f32[512,2560]{1,0:T(8,128)S(1)}) fusion(bf16[2560,128]{1,0:T(8,128)(2,1)S(1)} %get-tuple-element.220, bf16[512,1024]{1,0:T(8,128)(2,1)} %get-tuple-element.219, s32[]{:T(128)S(6)} %select_n.63, s32[512]{0:T(512)} %get-tuple-element.223, s32[2560]{0:T(1024)S(1)} %get-tuple-element.224, ...), kind=kOutput, calls=%fused_computation.50.clone.1 | convolution fusion | flops 344718848 | bytes 6059012 | tf_op jit(solution)/shard_map/while/body/eval_jaxpr/dot_general | solution.py:53
  172.9 2.3 %copy-done.1 = f32[512,2560]{1,0:T(8,128)} copy-done((f32[512,2560]{1,0:T(8,128)}, f32[512,2560]{1,0:T(8,128)S(1)}, u32[]{:S(2)}) %copy-start.1) | copy-done | bytes 5242904 | tf_op jit(solution)/shard_map/while
  177.4 3.5 %fusion.47 = bf16[8,512,128]{2,1,0:T(8,128)(2,1)S(1)} fusion(bf16[8,512,128]{2,1,0:T(8,128)(2,1)S(1)} %get-tuple-element.200, s32[]{:T(128)} %get-tuple-element.199, bf16[2560,128]{1,0:T(8,128)(2,1)S(1)} %get-tuple-element.221, f32[512,2560]{1,0:T(8,128)} %copy-done.1, f32[512]{0:T(512)S(1)} %get-tuple-element.182, f32[512]{0:T(512)S(1)} %fusion.46), kind=kOutput, calls=%fused_computation.13.clone.1 | convolution fusion | flops 338296832 | bytes 6033412 | tf_op jit(solution)/shard_map/while/body/eval_jaxpr/dot_general | solution.py:64
  182.2 3.1 %fusion.45 = (f32[512]{0:T(512)S(1)}, f32[512,2560]{1,0:T(8,128)S(1)}) fusion(bf16[2560,128]{1,0:T(8,128)(2,1)S(1)} %get-tuple-element.220, bf16[512,1024]{1,0:T(8,128)(2,1)} %get-tuple-element.219, s32[]{:T(128)S(6)} %select_n.63, s32[512]{0:T(512)} %get-tuple-element.223, s32[2560]{0:T(1024)S(1)} %get-tuple-element.224, ...), kind=kOutput, calls=%fused_computation.50.clone.1 | convolution fusion | flops 344718848 | bytes 6059012 | tf_op jit(solution)/shard_map/while/body/eval_jaxpr/dot_general | solution.py:53
  189.7 3.5 %fusion.47 = bf16[8,512,128]{2,1,0:T(8,128)(2,1)S(1)} fusion(bf16[8,512,128]{2,1,0:T(8,128)(2,1)S(1)} %get-tuple-element.200, s32[]{:T(128)} %get-tuple-element.199, bf16[2560,128]{1,0:T(8,128)(2,1)S(1)} %get-tuple-element.221, f32[512,2560]{1,0:T(8,128)} %copy-done.1, f32[512]{0:T(512)S(1)} %get-tuple-element.182, f32[512]{0:T(512)S(1)} %fusion.46), kind=kOutput, calls=%fused_computation.13.clone.1 | convolution fusion | flops 338296832 | bytes 6033412 | tf_op jit(solution)/shard_map/while/body/eval_jaxpr/dot_general | solution.py:64
  (89 shorter events, 68.7 us)
Async XLA Ops:
  0.6 0.9 copy-start
  2.2 34.8 %all-to-all-start.1 = ((bf16[64,8,128]{2,0,1:T(8,128)(2,1)}), bf16[64,8,128]{2,0,1:T(8,128)(2,1)S(1)}, u32[]{:S(2)}, u32[]{:S(2)}) async-start(bf16[64,8,128]{2,0,1:T(8,128)(2,1)} %copy_bitcast_fusion.1), calls=%async_computation.1 | async-start | bytes 262144 | tf_op jit(solution)/shard_map/all_to_all | solution.py:19
  7.4 9.3 %collective-permute-start.4 = (s32[512]{0:T(512)}, s32[512]{0:T(512)S(1)}, u32[]{:S(2)}, u32[]{:S(2)}) collective-permute-start(s32[512]{0:T(512)} %param.11), channel_id=1, source_target_pairs={{0,8},{8,16},{16,24},{24,32},{32,40},{40,48},{48,56},{56,64},{64,7... | collective-permute-start | bytes 6152 | tf_op jit(solution)/shard_map/ppermute | solution.py:13
  16.7 9.1 %collective-permute-start.5 = (s32[512]{0:T(512)S(1)}, s32[512]{0:T(512)S(1)}, u32[]{:S(2)}, u32[]{:S(2)}) collective-permute-start(s32[512]{0:T(512)S(1)} %collective-permute-done.4), channel_id=1, source_target_pairs={{0,8},{8,16},{16,24},{24,32},{32,40},{40,48},{48,56},{56,64},{64,7... | collective-permute-start | bytes 6152 | tf_op jit(solution)/shard_map/ppermute | solution.py:13
  25.9 9.2 %collective-permute-start.6 = (s32[512]{0:T(512)S(1)}, s32[512]{0:T(512)S(1)}, u32[]{:S(2)}, u32[]{:S(2)}) collective-permute-start(s32[512]{0:T(512)S(1)} %collective-permute-done.5), channel_id=1, source_target_pairs={{0,8},{8,16},{16,24},{24,32},{32,40},{40,48},{48,56},{56,64},{64,7... | collective-permute-start | bytes 6152 | tf_op jit(solution)/shard_map/ppermute | solution.py:13
  35.1 9.1 %collective-permute-start.7 = (s32[512]{0:T(512)S(1)}, s32[512]{0:T(512)S(1)}, u32[]{:S(2)}, u32[]{:S(2)}) collective-permute-start(s32[512]{0:T(512)S(1)} %collective-permute-done.6), channel_id=1, source_target_pairs={{0,8},{8,16},{16,24},{24,32},{32,40},{40,48},{48,56},{56,64},{64,7... | collective-permute-start | bytes 6152 | tf_op jit(solution)/shard_map/ppermute | solution.py:13
  37.0 12.4 %all-to-all-start = ((bf16[64,8,128]{2,0,1:T(8,128)(2,1)}), bf16[64,8,128]{2,0,1:T(8,128)(2,1)S(1)}, u32[]{:S(2)}, u32[]{:S(2)}) async-start(bf16[64,8,128]{2,0,1:T(8,128)(2,1)} %copy_bitcast_fusion.2), calls=%async_computation | async-start | bytes 262144 | tf_op jit(solution)/shard_map/all_to_all | solution.py:18
  44.2 11.9 %collective-permute-start.8 = (bf16[512,128]{1,0:T(8,128)(2,1)S(1)}, bf16[512,128]{1,0:T(8,128)(2,1)S(1)}, u32[]{:S(2)}, u32[]{:S(2)}) collective-permute-start(bf16[512,128]{1,0:T(8,128)(2,1)S(1)} %bitcast.41), channel_id=1, source_target_pairs={{0,8},{8,16},{16,24},{24,32},{32,40},{40,48},{48,56},{56,64},{64,7... | collective-permute-start | bytes 393224 | tf_op jit(solution)/shard_map/ppermute | solution.py:13
  49.4 11.2 %collective-permute-start = (bf16[512,128]{1,0:T(8,128)(2,1)S(1)}, bf16[512,128]{1,0:T(8,128)(2,1)S(1)}, u32[]{:S(2)}, u32[]{:S(2)}) collective-permute-start(bf16[512,128]{1,0:T(8,128)(2,1)S(1)} %bitcast.43), channel_id=1, source_target_pairs={{0,8},{8,16},{16,24},{24,32},{32,40},{40,48},{48,56},{56,64},{64,7... | collective-permute-start | bytes 393224 | tf_op jit(solution)/shard_map/ppermute | solution.py:13
  56.0 11.5 %collective-permute-start.9 = (bf16[512,128]{1,0:T(8,128)(2,1)S(1)}, bf16[512,128]{1,0:T(8,128)(2,1)S(1)}, u32[]{:S(2)}, u32[]{:S(2)}) collective-permute-start(bf16[512,128]{1,0:T(8,128)(2,1)S(1)} %collective-permute-done.8), channel_id=1, source_target_pairs={{0,8},{8,16},{16,24},{24,32},{32,40},{40,48},{48,56},{56,64},{64,7... | collective-permute-start | bytes 393224 | tf_op jit(solution)/shard_map/ppermute | solution.py:13
  60.5 11.5 %collective-permute-start.1 = (bf16[512,128]{1,0:T(8,128)(2,1)S(1)}, bf16[512,128]{1,0:T(8,128)(2,1)S(1)}, u32[]{:S(2)}, u32[]{:S(2)}) collective-permute-start(bf16[512,128]{1,0:T(8,128)(2,1)S(1)} %collective-permute-done), channel_id=1, source_target_pairs={{0,8},{8,16},{16,24},{24,32},{32,40},{40,48},{48,56},{56,64},{64,7... | collective-permute-start | bytes 393224 | tf_op jit(solution)/shard_map/ppermute | solution.py:13
  67.5 11.7 %collective-permute-start.10 = (bf16[512,128]{1,0:T(8,128)(2,1)S(1)}, bf16[512,128]{1,0:T(8,128)(2,1)S(1)}, u32[]{:S(2)}, u32[]{:S(2)}) collective-permute-start(bf16[512,128]{1,0:T(8,128)(2,1)S(1)} %collective-permute-done.9), channel_id=1, source_target_pairs={{0,8},{8,16},{16,24},{24,32},{32,40},{40,48},{48,56},{56,64},{64,7... | collective-permute-start | bytes 393224 | tf_op jit(solution)/shard_map/ppermute | solution.py:13
  72.0 11.4 %collective-permute-start.2 = (bf16[512,128]{1,0:T(8,128)(2,1)S(1)}, bf16[512,128]{1,0:T(8,128)(2,1)S(1)}, u32[]{:S(2)}, u32[]{:S(2)}) collective-permute-start(bf16[512,128]{1,0:T(8,128)(2,1)S(1)} %collective-permute-done.1), channel_id=1, source_target_pairs={{0,8},{8,16},{16,24},{24,32},{32,40},{40,48},{48,56},{56,64},{64,7... | collective-permute-start | bytes 393224 | tf_op jit(solution)/shard_map/ppermute | solution.py:13
  79.3 11.7 %collective-permute-start.11 = (bf16[512,128]{1,0:T(8,128)(2,1)S(1)}, bf16[512,128]{1,0:T(8,128)(2,1)S(1)}, u32[]{:S(2)}, u32[]{:S(2)}) collective-permute-start(bf16[512,128]{1,0:T(8,128)(2,1)S(1)} %collective-permute-done.10), channel_id=1, source_target_pairs={{0,8},{8,16},{16,24},{24,32},{32,40},{40,48},{48,56},{56,64},{64,7... | collective-permute-start | bytes 393224 | tf_op jit(solution)/shard_map/ppermute | solution.py:13
  83.4 11.4 %collective-permute-start.3 = (bf16[512,128]{1,0:T(8,128)(2,1)S(1)}, bf16[512,128]{1,0:T(8,128)(2,1)S(1)}, u32[]{:S(2)}, u32[]{:S(2)}) collective-permute-start(bf16[512,128]{1,0:T(8,128)(2,1)S(1)} %collective-permute-done.2), channel_id=1, source_target_pairs={{0,8},{8,16},{16,24},{24,32},{32,40},{40,48},{48,56},{56,64},{64,7... | collective-permute-start | bytes 393224 | tf_op jit(solution)/shard_map/ppermute | solution.py:13
  99.2 2.3 %copy-start.1 = (f32[512,2560]{1,0:T(8,128)}, f32[512,2560]{1,0:T(8,128)S(1)}, u32[]{:S(2)}) copy-start(f32[512,2560]{1,0:T(8,128)S(1)} %get-tuple-element.181) | copy-start | bytes 15728644 | tf_op jit(solution)/shard_map/while
  111.5 2.3 %copy-start.1 = (f32[512,2560]{1,0:T(8,128)}, f32[512,2560]{1,0:T(8,128)S(1)}, u32[]{:S(2)}) copy-start(f32[512,2560]{1,0:T(8,128)S(1)} %get-tuple-element.181) | copy-start | bytes 15728644 | tf_op jit(solution)/shard_map/while
  123.8 2.3 %copy-start.1 = (f32[512,2560]{1,0:T(8,128)}, f32[512,2560]{1,0:T(8,128)S(1)}, u32[]{:S(2)}) copy-start(f32[512,2560]{1,0:T(8,128)S(1)} %get-tuple-element.181) | copy-start | bytes 15728644 | tf_op jit(solution)/shard_map/while
  136.1 2.3 %copy-start.1 = (f32[512,2560]{1,0:T(8,128)}, f32[512,2560]{1,0:T(8,128)S(1)}, u32[]{:S(2)}) copy-start(f32[512,2560]{1,0:T(8,128)S(1)} %get-tuple-element.181) | copy-start | bytes 15728644 | tf_op jit(solution)/shard_map/while
  148.4 2.3 %copy-start.1 = (f32[512,2560]{1,0:T(8,128)}, f32[512,2560]{1,0:T(8,128)S(1)}, u32[]{:S(2)}) copy-start(f32[512,2560]{1,0:T(8,128)S(1)} %get-tuple-element.181) | copy-start | bytes 15728644 | tf_op jit(solution)/shard_map/while
  160.6 2.3 %copy-start.1 = (f32[512,2560]{1,0:T(8,128)}, f32[512,2560]{1,0:T(8,128)S(1)}, u32[]{:S(2)}) copy-start(f32[512,2560]{1,0:T(8,128)S(1)} %get-tuple-element.181) | copy-start | bytes 15728644 | tf_op jit(solution)/shard_map/while
  172.9 2.3 %copy-start.1 = (f32[512,2560]{1,0:T(8,128)}, f32[512,2560]{1,0:T(8,128)S(1)}, u32[]{:S(2)}) copy-start(f32[512,2560]{1,0:T(8,128)S(1)} %get-tuple-element.181) | copy-start | bytes 15728644 | tf_op jit(solution)/shard_map/while
  185.2 2.3 %copy-start.1 = (f32[512,2560]{1,0:T(8,128)}, f32[512,2560]{1,0:T(8,128)S(1)}, u32[]{:S(2)}) copy-start(f32[512,2560]{1,0:T(8,128)S(1)} %get-tuple-element.181) | copy-start | bytes 15728644 | tf_op jit(solution)/shard_map/while
where the time goes:
time: 196 us; the launch traced here: 194 us
  waiting for transfers between devices  55.4 us (28%)
  matrix products  52.2 us (27%)
  local copies, waits for them, and re-layouts  39.1 us (20%)
  starting transfers between devices  33.8 us (17%)
  other arithmetic  7.56 us (4%)
  loops' own time  5.47 us (3%)
    ppermute x12, waiting for transfers between devices, passed_along(): lax.ppermute(value, axis, [(source, source + steps) for source in range(i...  52.2 us
    dot_general x8, matrix products, one_head(): jnp.dot(weights, value_cat, preferred_element_type=jnp.float32)  27.7 us
    dot_general x8, matrix products, one_head(): lax.dot_general(query_head, key_cat, (((1,), (1,)), ((), ())), preferred_...  24.5 us
    ppermute x12, starting transfers between devices, passed_along(): lax.ppermute(value, axis, [(source, source + steps) for source in range(i...  22.9 us
    while x16, local copies, waits for them, and re-layouts  18.4 us
    dynamic_update_slice x8, local copies, waits for them, and re-layouts, body(): lax.map(one_head, jnp.arange(local_heads, dtype=jnp.int32))  10.8 us
    reduce_sum x8, other arithmetic, one_head(): row_total = jnp.sum(exp_terms, 1)  6.72 us
    all_to_all x1, starting transfers between devices, body(): lax.all_to_all(key_rows, 'head', split_axis=1, concat_axis=0, tiled=True)  5.65 us
  transfers between devices with their start and end apart: 14, of which 13 were waited for; matrix products, arithmetic and copies ran while one was open for 2% of the time, Pallas kernels for 0%

commit v1 on v0

v1 whole, which is shorter than its diff:
```python
import functools

import jax
import jax.numpy as jnp
from jax import lax
from jax.experimental import pallas as pl
from jax.experimental.pallas import tpu as pltpu
from jax.sharding import PartitionSpec as P

HD = 128
BLOCK = 512
SLOTS = 5
GROUP = 8
HEADS = 8
ROWS = BLOCK // GROUP
DROWS = 16
KROWS = BLOCK + DROWS
CHIP = 2
YSIZE = 8
PLANE = CHIP * YSIZE
SCALE = float(HD**-0.5)
SCALE_LOG2 = float(HD**-0.5 * 1.4426950408889634)
HIDE = -(2.0**100)
MESH = pl.DeviceIdType.MESH
F32 = jnp.float32
BF16 = jnp.bfloat16
CONTRACT_LAST = (((1,), (1,)), ((), ()))


def lane_max(scores):
    best = scores[:, :HD]
    for j in range(1, scores.shape[1] // HD):
        best = jnp.maximum(best, scores[:, j * HD : (j + 1) * HD])
    return best


def kernel(
    blocks, q_hbm, k_hbm, v_hbm, mask_ref, depth_ref, o_ref, l_ref,
    qb, kb, vb, stage_k, stage_v, kx, qx, sc, mx, acc,
    k_send, k_recv, v_send, v_recv, local_sem,
):
    s = lax.axis_index("seq")
    g = lax.axis_index("head")
    core = s % CHIP
    other = s + 1 - 2 * core
    y = (s // CHIP) % YSIZE
    last_y = y == YSIZE - 1
    has_next = s < blocks - CHIP
    has_prev = s >= CHIP
    to_plane = last_y & has_next
    from_plane = last_y & (s >= PLANE)
    cross_in = (y == 0) & (s >= PLANE)

    def at_seq(t):
        return {"seq": t, "head": g}

    barrier = pltpu.get_barrier_semaphore()
    for j in range(1, GROUP):
        pl.semaphore_signal(
            barrier, inc=1, device_id={"seq": s, "head": (g + j) % GROUP}, device_id_type=MESH
        )
    pl.semaphore_signal(barrier, inc=1, device_id=at_seq(other), device_id_type=MESH)
    partners = (
        (has_next, s + CHIP),
        (has_prev, s - CHIP),
        (to_plane, s + PLANE),
        (from_plane, s - PLANE),
        (from_plane, s - PLANE + CHIP),
        (cross_in, s + PLANE - CHIP),
    )
    expected = jnp.int32(GROUP)
    for cond, target in partners:
        expected = expected + jnp.where(cond, 1, 0)

        @pl.when(cond)
        def _(target=target):
            pl.semaphore_signal(barrier, inc=1, device_id=at_seq(target), device_id_type=MESH)

    q_copy = pltpu.make_async_copy(q_hbm, qb, local_sem.at[2])
    q_copy.start()
    depth = depth_ref[...]
    depth_rows = jnp.concatenate(
        [depth[:, i * HD : (i + 1) * HD] for i in range(BLOCK // HD)]
        + [jnp.zeros((DROWS - BLOCK // HD, HD), jnp.int32)],
        0,
    )
    kb[0, BLOCK:] = depth_rows.astype(F32).astype(BF16)
    pl.semaphore_wait(barrier, expected)

    mine = pl.ds(pl.multiple_of(g * ROWS, ROWS), ROWS)

    def spread(src, dst, send, recv, lsem):
        copies = []
        for j in range(1, GROUP):
            t = (g + j) % GROUP
            copy = pltpu.make_async_remote_copy(
                src_ref=src.at[:, pl.ds(pl.multiple_of(t * HD, HD), HD)],
                dst_ref=dst.at[0, mine],
                send_sem=send.at[j - 1],
                recv_sem=recv.at[j - 1],
                device_id={"seq": s, "head": t},
                device_id_type=MESH,
            )
            copy.start()
            copies.append(copy)
        own = pltpu.make_async_copy(
            src.at[:, pl.ds(pl.multiple_of(g * HD, HD), HD)], dst.at[0, mine], lsem
        )
        own.start()
        return copies, own

    k_spread, k_own = spread(k_hbm, kb, k_send, k_recv, local_sem.at[0])
    v_spread, v_own = spread(v_hbm, vb, v_send, v_recv, local_sem.at[1])

    def moves(buf, stage, send, recv):
        def move(src, dst, i, target):
            return pltpu.make_async_remote_copy(
                src_ref=src,
                dst_ref=dst,
                send_sem=send.at[i],
                recv_sem=recv.at[i],
                device_id=at_seq(target),
                device_id_type=MESH,
            )

        return dict(
            hop1=move(buf.at[0], buf.at[2], 7, s + CHIP),
            hop2=move(buf.at[2], buf.at[4], 9, s + CHIP),
            plane=move(buf.at[2], stage, 11, s + PLANE),
            cross=move(stage, buf.at[4], 9, s - PLANE + CHIP),
            one_a=move(buf.at[0], buf.at[1], 8, other),
            one_b=move(buf.at[2], buf.at[1], 8, other),
            three_a=move(buf.at[2], buf.at[3], 10, other),
            three_b=move(buf.at[4], buf.at[3], 10, other),
        )

    km = moves(kb, stage_k, k_send, k_recv)
    vm = moves(vb, stage_v, v_send, v_recv)

    def when(cond, act):
        @pl.when(cond)
        def _():
            act()

    core0, core1 = core == 0, core == 1
    fwd = has_prev & has_next & jnp.logical_not(last_y)
    fwd_plane = to_plane

    def send_first(m):
        when(has_next, m["hop1"].start)
        when(core0, m["one_a"].start)

    def pass_second(m):
        when(has_prev, m["hop1"].wait_recv)
        when(fwd, m["hop2"].start)
        when(fwd_plane, m["plane"].start)
        when(core0 & has_prev, m["three_a"].start)
        when(core1 & has_prev, m["one_b"].start)

    def pass_fourth(m):
        when(s >= 4, m["hop2"].wait_recv)
        when(core1 & (s >= 4), m["three_b"].start)

    def pass_plane(m):
        def act():
            m["plane"].wait_recv()
            m["cross"].start()

        when(from_plane, act)

    q_copy.wait()
    sub = lax.broadcasted_iota(jnp.int32, (HD, BLOCK), 0)
    q_side = jnp.where(
        sub < 8, jnp.where(sub > depth, HIDE, 0.0), jnp.where(sub == 8, 1.0, 0.0)
    ).astype(F32)
    qx[...] = q_side.T.astype(BF16)

    def key_side(slot):
        rows = kb[slot, BLOCK:, :].astype(F32)
        line = jnp.concatenate([rows[i : i + 1] for i in range(BLOCK // HD)], 1)
        off = jnp.where(mask_ref[0, slot] > 0, 0.0, HIDE).astype(F32)
        side = jnp.where(
            sub < 8, jnp.where(sub.astype(F32) == line, 1.0, 0.0), jnp.where(sub == 8, off, 0.0)
        ).astype(F32)
        kx[...] = side.T.astype(BF16)

    half = BLOCK // 2

    def own_scores():
        row = lax.broadcasted_iota(jnp.int32, (half, half), 0)
        col = lax.broadcasted_iota(jnp.int32, (half, half), 1)

        def heads(i, carry):
            for k in range(4):
                h = i * 4 + k
                cols = pl.ds(pl.multiple_of(h * HD, HD), HD)
                for t in range(2):
                    rs = slice(t * half, (t + 1) * half)
                    n = (t + 1) * half
                    scores = lax.dot_general(
                        qb[rs, cols], kb[0, :n], CONTRACT_LAST, preferred_element_type=F32
                    )
                    diag = jnp.where(col <= row, scores[:, n - half :], HIDE)
                    sc[h, 0, rs, n - half : n] = diag
                    best = lane_max(diag)
                    if t:
                        sc[h, 0, rs, : n - half] = scores[:, : n - half]
                        best = jnp.maximum(best, lane_max(scores[:, : n - half]))
                    mx[h, rs] = best
            return carry

        lax.fori_loop(0, HEADS // 4, heads, 0)

    def slot_scores(slot):
        key_side(slot)

        def heads(i, carry):
            keys = jnp.concatenate([kb[slot, :BLOCK], kx[...]], 1)
            for k in range(4):
                h = i * 4 + k
                cols = pl.ds(pl.multiple_of(h * HD, HD), HD)
                query = jnp.concatenate([qb[:, cols], qx[...]], 1)
                scores = lax.dot_general(query, keys, CONTRACT_LAST, preferred_element_type=F32)
                sc[h, slot] = scores
                mx[h] = jnp.maximum(mx[h], lane_max(scores))
            return carry

        lax.fori_loop(0, HEADS // 4, heads, 0)

    def wait_spread(copies, own):
        own.wait()
        for copy in copies:
            copy.wait_recv()

    wait_spread(k_spread, k_own)
    send_first(km)
    own_scores()
    pass_second(km)
    wait_spread(v_spread, v_own)
    send_first(vm)

    for slot in range(1, SLOTS):

        @pl.when(s < slot)
        def _(slot=slot):
            vb[slot] = jnp.zeros((BLOCK, HD), BF16)

            def fill(h, carry):
                sc[h, slot] = jnp.full((BLOCK, BLOCK), HIDE, F32)
                return carry

            lax.fori_loop(0, HEADS, fill, 0)

    when(core1, km["one_a"].wait_recv)
    second, third, fourth, fifth = 2 - core, 1 + core, 4 - core, 3 + core
    when(s >= second, lambda: slot_scores(second))
    when(core0 & (s >= 1), km["one_a"].wait_recv)
    when(s >= third, lambda: slot_scores(third))
    pass_fourth(km)
    when(core1 & (s >= 3), km["three_a"].wait_recv)
    when(s >= fourth, lambda: slot_scores(fourth))
    pass_plane(km)
    pass_second(vm)
    when(core0 & (s >= 3), km["three_a"].wait_recv)
    when(s >= fifth, lambda: slot_scores(fifth))
    when(s >= 1, vm["one_a"].wait_recv)

    def attend(slots, first, last):
        def heads(i, carry):
            for k in range(2):
                h = i * 2 + k
                cols = pl.ds(pl.multiple_of(h * HD, HD), HD)
                for t in range(2):
                    rs = slice(t * half, (t + 1) * half)
                    if first:
                        top = jnp.max(mx[h, rs], axis=1, keepdims=True)
                        mx[h, rs] = jnp.broadcast_to(top, (half, HD))
                        total = jnp.zeros((half, 2 * HD), F32)
                    else:
                        top = mx[h, rs][:, :1]
                        total = acc[h, rs]
                    for slot in slots:
                        n = BLOCK if slot else (t + 1) * half
                        terms = jnp.exp2((sc[h, slot, rs, :n] - top) * SCALE_LOG2)
                        values = jnp.concatenate([vb[slot, :n], jnp.ones((n, HD), BF16)], 1)
                        total = total + jnp.dot(
                            terms.astype(BF16), values, preferred_element_type=F32
                        )
                    if last:
                        sums = total[:, HD:]
                        o_ref[rs, cols] = (total[:, :HD] / sums).astype(BF16)
                        logs = top * SCALE + jnp.log(sums[:, :1])
                        l_ref[pl.ds(h, 1), rs] = logs.reshape(1, half)
                    else:
                        acc[h, rs] = total
            return carry

        lax.fori_loop(0, HEADS // 2, heads, 0)

    attend((0, 1, 2), True, False)
    pass_fourth(vm)
    pass_plane(vm)
    when(s >= 3, vm["three_a"].wait_recv)
    attend((3, 4), False, True)

    for copy in k_spread + v_spread:
        copy.wait_send()
    for m in (km, vm):
        when(has_next, m["hop1"].wait_send)
        when(fwd, m["hop2"].wait_send)
        when(fwd_plane, m["plane"].wait_send)
        when(from_plane, m["cross"].wait_send)
        when(core0 | has_prev, m["one_a"].wait_send)
        when((core0 & has_prev) | (core1 & (s >= 4)), m["three_a"].wait_send)


def solution(mesh):
    blocks = mesh.shape["seq"]

    def body(query_rows, key_rows, value_rows, tree_mask, token_depth):
        vmem = pl.BlockSpec(memory_space=pltpu.VMEM)
        anywhere = pl.BlockSpec(memory_space=pl.ANY)
        sems = pltpu.SemaphoreType.DMA
        return pl.pallas_call(
            functools.partial(kernel, blocks),
            out_shape=(
                jax.ShapeDtypeStruct((BLOCK, HEADS * HD), BF16),
                jax.ShapeDtypeStruct((HEADS, BLOCK), F32),
            ),
            in_specs=[anywhere] * 3 + [pl.BlockSpec(memory_space=pltpu.SMEM), vmem],
            out_specs=(vmem, vmem),
            scratch_shapes=[
                pltpu.VMEM((BLOCK, HEADS * HD), BF16),
                pltpu.VMEM((SLOTS, KROWS, HD), BF16),
                pltpu.VMEM((SLOTS, BLOCK, HD), BF16),
                pltpu.VMEM((KROWS, HD), BF16),
                pltpu.VMEM((BLOCK, HD), BF16),
                pltpu.VMEM((BLOCK, HD), BF16),
                pltpu.VMEM((BLOCK, HD), BF16),
                pltpu.VMEM((HEADS, SLOTS, BLOCK, BLOCK), F32),
                pltpu.VMEM((HEADS, BLOCK, HD), F32),
                pltpu.VMEM((HEADS, BLOCK, 2 * HD), F32),
                sems((12,)), sems((12,)), sems((12,)), sems((12,)), sems((3,)),
            ],
            compiler_params=pltpu.CompilerParams(
                collective_id=0, has_side_effects=True, vmem_limit_bytes=60 * 2**20
            ),
        )(query_rows, key_rows, value_rows, tree_mask, token_depth.reshape(1, BLOCK))

    return jax.shard_map(
        body,
        mesh=mesh,
        in_specs=(
            P("seq", "head"),
            P(("seq", "head"), None),
            P(("seq", "head"), None),
            P("seq", None),
            P("seq"),
        ),
        out_specs=(P("seq", "head"), P("head", "seq")),
        check_vma=False,
    )
```

time: 196 us -> 44.4 us (0.23)
  the two profiles are of different devices: /device:TPU:256 before, /device:TPU:128 now
where the time goes in v1:
time: 44.4 us; the launch traced here: 44.2 us
  Pallas kernels  40.7 us (92%)
  local copies, waits for them, and re-layouts  2.88 us (6%)
  between operations  0.65 us (1%)
    pallas_call x1, Pallas kernels, body(): pl.pallas_call(functools.partial(kernel, blocks), out_shape=(jax.ShapeDty...  40.7 us
    unnamed x4, local copies, waits for them, and re-layouts  2.88 us

profile of v1, /device:TPU:128, one launch (start us, length us, event | category | flops | bytes accessed | tf_op | source)
XLA Modules:
  0.0 44.2 jit_solution(16771368975179547447)
XLA Ops:
  0.6 40.7 %shard_map.68 = (bf16[512,1024]{1,0:T(8,128)(2,1)}, f32[8,512]{1,0:T(8,128)}) custom-call(bf16[512,1024]{1,0:T(8,128)(2,1)} %q_hbm.1, bf16[64,1024]{1,0:T(8,128)(2,1)} %k_hbm.1, bf16[64,1024]{1,0:T(8,128)(2,1)} %v_hbm.1, s32[1,5]{1,0:T(1,128)} %mask_ref.1, s32[1,512]{1,0:T(1,128)} %bitcast.1), custom_call_target="tpu_custom_call" | custom-call | tf_op jit(solution)/shard_map/pallas_call | solution.py:324
  41.3 0.0 copy-start
  41.3 2.3 %copy.9 = bf16[512,1024]{1,0:T(8,128)(2,1)} copy(bf16[512,1024]{1,0:T(8,128)(2,1)} %get-tuple-element.4) | data formatting | bytes 2097152
  43.6 0.0 copy-done
  43.6 0.6 %copy.10 = f32[8,512]{1,0:T(8,128)} copy(f32[8,512]{1,0:T(8,128)S(1)} %copy-done) | data formatting | bytes 32768
Async XLA Ops:
  41.3 2.3 %copy-start = (f32[8,512]{1,0:T(8,128)S(1)}, f32[8,512]{1,0:T(8,128)}, u32[]{:S(2)}) copy-start(f32[8,512]{1,0:T(8,128)} %get-tuple-element.5) | copy-start | bytes 49156

commit v2 on v1

v2 whole, which is shorter than its diff:
```python
import functools

import jax
import jax.numpy as jnp
from jax import lax
from jax.experimental import pallas as pl
from jax.experimental.pallas import tpu as pltpu
from jax.sharding import PartitionSpec as P

HD = 128
BLOCK = 512
SLOTS = 5
GROUP = 8
HEADS = 8
PER_BODY = 8
PIECES = 4
ROWS = BLOCK // GROUP
HALF = BLOCK // 2
DROWS = 16
KROWS = BLOCK + DROWS
CHIP = 2
YSIZE = 8
PLANE = CHIP * YSIZE
SCALE = float(HD**-0.5)
SCALE_LOG2 = float(HD**-0.5 * 1.4426950408889634)
HIDE = -(2.0**100)
MESH = pl.DeviceIdType.MESH
F32 = jnp.float32
BF16 = jnp.bfloat16
CONTRACT_LAST = (((1,), (1,)), ((), ()))


def lane_max(scores):
    best = scores[:, :HD]
    for j in range(1, scores.shape[1] // HD):
        best = jnp.maximum(best, scores[:, j * HD : (j + 1) * HD])
    return best


def kernel(
    blocks, q_hbm, k_hbm, v_hbm, mask_hbm, depth_hbm, o_hbm, l_ref,
    mask_ref, depth_ref, k_in, v_in, ob, qb, kb, vb, kx, qx, sc, mx, tops, acc,
    k_send, k_recv, v_send, v_recv, local_sem,
):
    s = lax.axis_index("seq")
    g = lax.axis_index("head")
    core = s % CHIP
    other = s + 1 - 2 * core
    y = (s // CHIP) % YSIZE
    last_y = y == YSIZE - 1
    has_next = s < blocks - CHIP
    has_prev = s >= CHIP
    core0, core1 = core == 0, core == 1
    skips = last_y & core0 & has_next
    hands_back = (y == 1) & core0 & (s >= PLANE)
    relayed = (y == 0) & core0 & has_prev
    passes = has_prev & has_next & jnp.logical_not(relayed)

    def at_seq(t):
        return {"seq": t, "head": g}

    barrier = pltpu.get_barrier_semaphore()
    for j in range(1, GROUP):
        pl.semaphore_signal(
            barrier, inc=1, device_id={"seq": s, "head": (g + j) % GROUP}, device_id_type=MESH
        )
    pl.semaphore_signal(barrier, inc=1, device_id=at_seq(other), device_id_type=MESH)
    partners = (
        (has_next, s + CHIP),
        (has_prev, s - CHIP),
        (skips, s + 2 * CHIP),
        (hands_back, s - 2 * CHIP),
        (core1 & has_next, s + CHIP - 1),
        (core0 & has_prev, s - CHIP + 1),
    )
    expected = jnp.int32(GROUP)
    for cond, target in partners:
        expected = expected + jnp.where(cond, 1, 0)

        @pl.when(cond)
        def _(target=target):
            pl.semaphore_signal(barrier, inc=1, device_id=at_seq(target), device_id_type=MESH)

    q_copy = pltpu.make_async_copy(q_hbm, qb, local_sem.at[2])
    mask_copy = pltpu.make_async_copy(mask_hbm, mask_ref, local_sem.at[3])
    depth_copy = pltpu.make_async_copy(depth_hbm, depth_ref, local_sem.at[4])
    k_in_copy = pltpu.make_async_copy(k_hbm, k_in, local_sem.at[7])
    v_in_copy = pltpu.make_async_copy(v_hbm, v_in, local_sem.at[8])
    depth_copy.start()
    mask_copy.start()
    k_in_copy.start()
    v_in_copy.start()
    q_copy.start()
    depth_copy.wait()
    mask_copy.wait()
    depth = depth_ref[...]
    depth_rows = jnp.concatenate(
        [depth[:, i * HD : (i + 1) * HD] for i in range(BLOCK // HD)]
        + [jnp.zeros((DROWS - BLOCK // HD, HD), jnp.int32)],
        0,
    )
    kb[0, BLOCK:] = depth_rows.astype(F32).astype(BF16)
    k_in_copy.wait()
    v_in_copy.wait()
    pl.semaphore_wait(barrier, expected)

    mine = pl.ds(pl.multiple_of(g * ROWS, ROWS), ROWS)

    def spread(src, dst, send, recv, lsem):
        copies = []
        for j in range(1, GROUP):
            t = (g + j) % GROUP
            copy = pltpu.make_async_remote_copy(
                src_ref=src.at[:, pl.ds(pl.multiple_of(t * HD, HD), HD)],
                dst_ref=dst.at[0, mine],
                send_sem=send.at[j - 1],
                recv_sem=recv.at[j - 1],
                device_id={"seq": s, "head": t},
                device_id_type=MESH,
            )
            copy.start()
            copies.append(copy)
        own = pltpu.make_async_copy(
            src.at[:, pl.ds(pl.multiple_of(g * HD, HD), HD)], dst.at[0, mine], lsem
        )
        own.start()
        return copies, own

    k_spread, k_own = spread(k_in, kb, k_send, k_recv, local_sem.at[0])
    v_spread, v_own = spread(v_in, vb, v_send, v_recv, local_sem.at[1])

    far = jnp.where(skips, 1, 0)
    ahead = s + CHIP + CHIP * far

    def moves(buf, send, recv, parts):
        def move(src, rows, dst, i, at, target):
            return pltpu.make_async_remote_copy(
                src_ref=buf.at[src, rows],
                dst_ref=buf.at[dst, rows],
                send_sem=send.at[i],
                recv_sem=recv.at[at],
                device_id=at_seq(target),
                device_id_type=MESH,
            )

        whole = pl.ds(0, buf.shape[1])
        each = list(enumerate(parts))
        return dict(
            one_a=move(0, whole, 1, 13, 13, other),
            one_b=move(2, whole, 1, 13, 13, other),
            three_a=move(2, whole, 3, 14, 14, other),
            four=move(3, whole, 4, 15, 15, other),
            hop1=[move(0, p, 2 + 2 * far, 7 + i, 7 + i + 2 * far, ahead) for i, p in each],
            hop2=[move(2, p, 4 - core, 9 + i, 9 + i + 2 * core, s + CHIP - core) for i, p in each],
            in3=[move(2, p, 3, 9 + i, 11 + i, s + CHIP) for i, p in each],
            in2=[move(0, p, 2, 7 + i, 7 + i, s + CHIP) for i, p in each],
            in4=[move(2, p, 4, 9 + i, 9 + i, s + CHIP) for i, p in each],
            back2=[move(4, p, 2, 11 + i, 7 + i, s - CHIP) for i, p in each],
        )

    km = moves(kb, k_send, k_recv, (pl.ds(0, HALF), pl.ds(HALF, KROWS - HALF)))
    vm = moves(vb, v_send, v_recv, (pl.ds(0, BLOCK),))

    def when(cond, act):
        @pl.when(cond)
        def _():
            act()

    def send_first(m):
        when(core0, m["one_a"].start)
        for copy in m["hop1"]:
            when(has_next, copy.start)

    def pass_second(m, later):
        for copy in m["in2"]:
            when(has_prev, copy.wait_recv)
        when(core0 & has_prev, m["three_a"].start)
        when(core1 & has_prev, m["one_b"].start)
        for copy in m["hop2"]:
            when(passes & jnp.logical_not(later), copy.start)

    def hand_back(m):
        for arrived, back in zip(m["in4"], m["back2"]):
            arrived.wait_recv()
            back.start()
        for copy in m["hop2"]:
            copy.start()

    def take_third(m):
        for copy in m["in3"]:
            copy.wait_recv()
        m["four"].start()

    def take_fourth(m):
        for copy in m["in4"]:
            when(core0 & (s >= 4) & jnp.logical_not(hands_back), copy.wait_recv)
        when(core1 & (s >= 4), m["four"].wait_recv)

    q_copy.wait()
    sub = lax.broadcasted_iota(jnp.int32, (HD, BLOCK), 0)
    q_side = jnp.where(
        sub < 8, jnp.where(sub > depth, HIDE, 0.0), jnp.where(sub == 8, 1.0, 0.0)
    ).astype(F32)
    qx[...] = q_side.T.astype(BF16)

    def key_side(slot):
        rows = kb[slot, BLOCK:, :].astype(F32)
        line = jnp.concatenate([rows[i : i + 1] for i in range(BLOCK // HD)], 1)
        off = jnp.where(mask_ref[0, slot] > 0, 0.0, HIDE).astype(F32)
        side = jnp.where(
            sub < 8, jnp.where(sub.astype(F32) == line, 1.0, 0.0), jnp.where(sub == 8, off, 0.0)
        ).astype(F32)
        kx[...] = side.T.astype(BF16)

    half = HALF

    def spread_max(scores):
        return jnp.broadcast_to(
            jnp.max(lane_max(scores), axis=1, keepdims=True), (scores.shape[0], HD)
        )

    def own_scores():
        row = lax.broadcasted_iota(jnp.int32, (half, half), 0)
        col = lax.broadcasted_iota(jnp.int32, (half, half), 1)

        def heads(i, carry):
            for k in range(PER_BODY):
                h = i * PER_BODY + k
                cols = pl.ds(pl.multiple_of(h * HD, HD), HD)
                for t in range(2):
                    rs = slice(t * half, (t + 1) * half)
                    n = (t + 1) * half
                    scores = lax.dot_general(
                        qb[rs, cols], kb[0, :n], CONTRACT_LAST, preferred_element_type=F32
                    )
                    diag = jnp.where(col <= row, scores[:, n - half :], HIDE)
                    sc[h, 0, rs, n - half : n] = diag
                    best = lane_max(diag)
                    if t:
                        sc[h, 0, rs, : n - half] = scores[:, : n - half]
                        best = jnp.maximum(best, lane_max(scores[:, : n - half]))
                    mx[h, rs] = spread_max(best)
            return carry

        lax.fori_loop(0, HEADS // PER_BODY, heads, 0)

    def slot_scores(slot):
        key_side(slot)

        def heads(i, carry):
            keys = jnp.concatenate([kb[slot, :BLOCK], kx[...]], 1)
            for k in range(PER_BODY):
                h = i * PER_BODY + k
                cols = pl.ds(pl.multiple_of(h * HD, HD), HD)
                query = jnp.concatenate([qb[:, cols], qx[...]], 1)
                scores = lax.dot_general(query, keys, CONTRACT_LAST, preferred_element_type=F32)
                sc[h, slot] = scores
                mx[h] = jnp.maximum(mx[h], spread_max(scores))
            return carry

        lax.fori_loop(0, HEADS // PER_BODY, heads, 0)

    def store_result(h, rs, sums, top):
        cols = pl.ds(pl.multiple_of(h * HD, HD), HD)
        ob[rs, cols] = (sums[:, :HD] / sums[:, HD:]).astype(BF16)
        logs = top * SCALE + jnp.log(sums[:, HD:])
        l_ref[pl.ds(h, 1), rs] = logs[:, :1].reshape(1, half)

    def out_copy(i):
        cols = pl.ds(pl.multiple_of(i * (HEADS * HD // 2), HEADS * HD // 2), HEADS * HD // 2)
        return pltpu.make_async_copy(ob.at[:, cols], o_hbm.at[:, cols], local_sem.at[5 + i])

    def absorb(slots, first=False, last=False):
        def heads(i, carry):
            for k in range(HEADS // 2):
                h = i * (HEADS // 2) + k
                for t in range(2):
                    rs = slice(t * half, (t + 1) * half)
                    top = mx[h, rs]
                    sums = None
                    for slot in slots:
                        n = (t + 1) * half if first else BLOCK
                        terms = jnp.concatenate(
                            [
                                jnp.exp2(
                                    (sc[h, slot, rs, j * HD : (j + 1) * HD] - top) * SCALE_LOG2
                                ).astype(BF16)
                                for j in range(n // HD)
                            ],
                            1,
                        )
                        values = jnp.concatenate([vb[slot, :n], jnp.ones((n, HD), BF16)], 1)
                        part = jnp.dot(terms, values, preferred_element_type=F32)
                        sums = part if sums is None else sums + part
                    if not first:
                        fade = jnp.exp2((tops[h, rs] - top) * SCALE_LOG2)
                        sums = acc[h, rs] * jnp.concatenate([fade, fade], 1) + sums
                    if last:
                        store_result(h, rs, sums, top)
                    else:
                        acc[h, rs] = sums
                        tops[h, rs] = top
            if last:
                out_copy(i).start()
            return carry

        lax.fori_loop(0, 2, heads, 0)

    def finish():
        def heads(i, carry):
            for k in range(HEADS // 2):
                h = i * (HEADS // 2) + k
                for t in range(2):
                    rs = slice(t * half, (t + 1) * half)
                    store_result(h, rs, acc[h, rs], tops[h, rs])
            out_copy(i).start()
            return carry

        lax.fori_loop(0, 2, heads, 0)

    def wait_spread(copies, own):
        own.wait()
        for copy in copies:
            copy.wait_recv()

    wait_spread(k_spread, k_own)
    send_first(km)
    own_scores()
    wait_spread(v_spread, v_own)
    send_first(vm)
    absorb((0,), first=True)

    @pl.when(s == 1)
    def _():
        vb[2] = jnp.zeros((BLOCK, HD), BF16)

        def fill(h, carry):
            sc[h, 2] = jnp.full((BLOCK, BLOCK), HIDE, F32)
            return carry

        lax.fori_loop(0, HEADS, fill, 0)

    def by_round(r, first_core, second_core):
        pick = jnp.int32(0)
        for i in range(len(first_core)):
            pick = jnp.where(r == i, jnp.where(core0, first_core[i], second_core[i]), pick)
        return pick

    def round_of(r, carry):
        def at(i, cond, act):
            when((r == i) & cond, act)

        plain0 = core0 & jnp.logical_not(relayed)
        at(0, core1, km["one_a"].wait_recv)
        at(1, jnp.logical_not(relayed), lambda: pass_second(km, hands_back))
        at(1, relayed, km["one_a"].wait_recv)
        at(2, hands_back, lambda: hand_back(km))
        at(2, relayed, lambda: pass_second(km, hands_back))
        at(2, jnp.logical_not(relayed), lambda: pass_second(vm, hands_back | skips))
        at(2, plain0 & (s >= 1), km["one_a"].wait_recv)
        at(3, hands_back, lambda: hand_back(vm))
        at(3, core0 & (s >= 4), lambda: take_third(km))
        at(3, core1 & (s >= 3), vm["three_a"].wait_recv)
        at(4, skips & passes, vm["hop2"][0].start)
        at(4, relayed, lambda: pass_second(vm, hands_back))
        at(5, core0 & (s >= 4), lambda: take_third(vm))
        pairs = (r == jnp.where(core1, 2, jnp.where(relayed, 4, 5))) & (s >= 1)
        when(pairs, vm["one_a"].wait_recv)
        when(pairs, lambda: absorb((1, 2)))
        thirds = ((r == 3) & core1 & (s >= 3)) | ((r == 5) & relayed)
        when(thirds, lambda: absorb((3,)))
        at(2, core1 & (s >= 3), km["three_a"].wait_recv)
        at(3, core1, lambda: take_fourth(km))
        at(4, core0, lambda: take_fourth(km))
        slot = by_round(
            r,
            tuple(jnp.where(relayed, i, j) for i, j in ((0, 0), (1, 2), (2, 1), (3, 3), (4, 4))),
            (1, 2, 3, 4, 0),
        )

        @pl.when((slot > 0) & (slot <= s))
        def _():
            slot_scores(slot)

        return carry

    lax.fori_loop(0, 6, round_of, 0)
    take_fourth(vm)
    both = core0 & jnp.logical_not(relayed)
    when((s >= 4) & both, lambda: absorb((3, 4), last=True))
    when((s >= 4) & jnp.logical_not(both), lambda: absorb((4,), last=True))
    when(s < 4, finish)
    for i in range(2):
        out_copy(i).wait()

    for copy in k_spread + v_spread:
        copy.wait_send()
    for m in (km, vm):
        for i in range(len(m["hop1"])):
            when(has_next, m["hop1"][i].wait_send)
            when(passes, m["hop2"][i].wait_send)
            when(hands_back, m["back2"][i].wait_send)
        when(core0 | has_prev, m["one_a"].wait_send)
        when(core0 & has_prev, m["three_a"].wait_send)
        when(core0 & (s >= 4), m["four"].wait_send)


def copy_out(a_in, l_in, a_out, l_out, a_buf, l_buf, sem_in, sem_out):
    rows = BLOCK // PIECES
    pieces = [pl.ds(i * rows, rows) for i in range(PIECES)]
    loads = [
        pltpu.make_async_copy(a_in.at[p], a_buf.at[p], sem_in.at[i]) for i, p in enumerate(pieces)
    ] + [pltpu.make_async_copy(l_in, l_buf, sem_in.at[PIECES])]
    stores = [
        pltpu.make_async_copy(a_buf.at[p], a_out.at[p], sem_out.at[i])
        for i, p in enumerate(pieces)
    ] + [pltpu.make_async_copy(l_buf, l_out, sem_out.at[PIECES])]
    for load in loads:
        load.start()
    for load, store in zip(loads, stores):
        load.wait()
        store.start()
    for store in stores:
        store.wait()


def solution(mesh):
    blocks = mesh.shape["seq"]

    def body(query_rows, key_rows, value_rows, tree_mask, token_depth):
        vmem = pl.BlockSpec(memory_space=pltpu.VMEM)
        anywhere = pl.BlockSpec(memory_space=pl.ANY)
        sems = pltpu.SemaphoreType.DMA
        results = pl.pallas_call(
            functools.partial(kernel, blocks),
            out_shape=(
                jax.ShapeDtypeStruct((BLOCK, HEADS * HD), BF16),
                jax.ShapeDtypeStruct((HEADS, BLOCK), F32),
            ),
            in_specs=[anywhere] * 5,
            out_specs=(anywhere, vmem),
            scratch_shapes=[
                pltpu.SMEM((1, SLOTS), jnp.int32),
                pltpu.VMEM((1, BLOCK), jnp.int32),
                pltpu.VMEM((ROWS, GROUP * HD), BF16),
                pltpu.VMEM((ROWS, GROUP * HD), BF16),
                pltpu.VMEM((BLOCK, HEADS * HD), BF16),
                pltpu.VMEM((BLOCK, HEADS * HD), BF16),
                pltpu.VMEM((SLOTS, KROWS, HD), BF16),
                pltpu.VMEM((SLOTS, BLOCK, HD), BF16),
                pltpu.VMEM((BLOCK, HD), BF16),
                pltpu.VMEM((BLOCK, HD), BF16),
                pltpu.VMEM((HEADS, SLOTS, BLOCK, BLOCK), F32),
                pltpu.VMEM((HEADS, BLOCK, HD), F32),
                pltpu.VMEM((HEADS, BLOCK, HD), F32),
                pltpu.VMEM((HEADS, BLOCK, 2 * HD), F32),
                sems((16,)), sems((16,)), sems((16,)), sems((16,)), sems((9,)),
            ],
            compiler_params=pltpu.CompilerParams(
                collective_id=0, has_side_effects=True, vmem_limit_bytes=60 * 2**20
            ),
        )(query_rows, key_rows, value_rows, tree_mask, token_depth.reshape(1, BLOCK))
        return pl.pallas_call(
            copy_out,
            out_shape=tuple(jax.ShapeDtypeStruct(r.shape, r.dtype) for r in results),
            in_specs=[anywhere] * 2,
            out_specs=(anywhere,) * 2,
            scratch_shapes=[
                pltpu.VMEM((BLOCK, HEADS * HD), BF16),
                pltpu.VMEM((HEADS, BLOCK), F32),
                sems((PIECES + 1,)),
                sems((PIECES + 1,)),
            ],
            compiler_params=pltpu.CompilerParams(vmem_limit_bytes=60 * 2**20),
        )(*results)

    return jax.shard_map(
        body,
        mesh=mesh,
        in_specs=(
            P("seq", "head"),
            P(("seq", "head"), None),
            P(("seq", "head"), None),
            P("seq", None),
            P("seq"),
        ),
        out_specs=(P("seq", "head"), P("head", "seq")),
        check_vma=False,
    )
```

time: 44.4 us -> 41.3 us (0.930)
  the two profiles are of different devices: /device:TPU:128 before, /device:TPU:256 now
where the time goes in v2:
time: 41.3 us; the launch traced here: 41.1 us
  Pallas kernels  40.5 us (98%)
  between operations  0.64 us (2%)
    pallas_call x1, Pallas kernels, body(): pl.pallas_call(functools.partial(kernel, blocks), out_shape=(jax.ShapeDty...  38.5 us
    pallas_call x1, Pallas kernels, body(): pl.pallas_call(copy_out, out_shape=tuple((jax.ShapeDtypeStruct(r.shape, r...  2 us

profile of v2, /device:TPU:256, one launch (start us, length us, event | category | flops | bytes accessed | tf_op | source)
XLA Modules:
  0.0 41.1 jit_solution(16280440062441660468)
XLA Ops:
  0.6 38.5 %shard_map.68 = (bf16[512,1024]{1,0:T(8,128)(2,1)}, f32[8,512]{1,0:T(8,128)}) custom-call(bf16[512,1024]{1,0:T(8,128)(2,1)} %q_hbm.1, bf16[64,1024]{1,0:T(8,128)(2,1)} %k_hbm.1, bf16[64,1024]{1,0:T(8,128)(2,1)} %v_hbm.1, s32[1,5]{1,0:T(1,128)} %mask_hbm.1, s32[1,512]{1,0:T(1,128)} %bitcast.1), custom_call_target="tpu_custom_call" | custom-call | tf_op jit(solution)/shard_map/pallas_call | solution.py:434
  39.1 2.0 %shard_map.69 = (bf16[512,1024]{1,0:T(8,128)(2,1)}, f32[8,512]{1,0:T(8,128)}) custom-call(bf16[512,1024]{1,0:T(8,128)(2,1)} %get-tuple-element.4.a_in, f32[8,512]{1,0:T(8,128)} %get-tuple-element.5.l_in), custom_call_target="tpu_custom_call" | custom-call | tf_op jit(solution)/shard_map/pallas_call | solution.py:463

commit v3 on v2

--- a/solution.py
+++ b/solution.py
@@ -200,8 +200,8 @@
     sub = lax.broadcasted_iota(jnp.int32, (HD, BLOCK), 0)
     q_side = jnp.where(
         sub < 8, jnp.where(sub > depth, HIDE, 0.0), jnp.where(sub == 8, 1.0, 0.0)
-    ).astype(F32)
-    qx[...] = q_side.T.astype(BF16)
+    ).astype(BF16)
+    qx[...] = q_side.T
 
     def key_side(slot):
         rows = kb[slot, BLOCK:, :].astype(F32)
@@ -209,8 +209,8 @@
         off = jnp.where(mask_ref[0, slot] > 0, 0.0, HIDE).astype(F32)
         side = jnp.where(
             sub < 8, jnp.where(sub.astype(F32) == line, 1.0, 0.0), jnp.where(sub == 8, off, 0.0)
-        ).astype(F32)
-        kx[...] = side.T.astype(BF16)
+        ).astype(BF16)
+        kx[...] = side.T
 
     half = HALF
 
@@ -271,11 +271,14 @@
         return pltpu.make_async_copy(ob.at[:, cols], o_hbm.at[:, cols], local_sem.at[5 + i])
 
     def absorb(slots, first=False, last=False):
+        per = HEADS
+        steps = 2
+
         def heads(i, carry):
-            for k in range(HEADS // 2):
-                h = i * (HEADS // 2) + k
-                for t in range(2):
-                    rs = slice(t * half, (t + 1) * half)
+            for k in range(per):
+                h = i * per + k
+                for t in range(steps):
+                    rs = slice(t * BLOCK // steps, (t + 1) * BLOCK // steps)
                     top = mx[h, rs]
                     sums = None
                     for slot in slots:
@@ -301,10 +304,11 @@
                         acc[h, rs] = sums
                         tops[h, rs] = top
             if last:
-                out_copy(i).start()
+                out_copy(0).start()
+                out_copy(1).start()
             return carry
 
-        lax.fori_loop(0, 2, heads, 0)
+        lax.fori_loop(0, HEADS // per, heads, 0)
 
     def finish():
         def heads(i, carry):

time: 41.3 us -> 40.5 us (0.981)
  Pallas kernels: 40.5 us -> 39.5 us
    pallas_call x1, Pallas kernels: 38.5 us -> 37.5 us  [body(): pl.pallas_call(functools.partial(kernel, blocks), out_shape=(jax.ShapeDty...]
where the time goes in v3:
time: 40.5 us; the launch traced here: 40.3 us
  Pallas kernels  39.5 us (98%)
  between operations  0.8 us (2%)
    pallas_call x1, Pallas kernels, body(): pl.pallas_call(functools.partial(kernel, blocks), out_shape=(jax.ShapeDty...  37.5 us
    pallas_call x1, Pallas kernels, body(): pl.pallas_call(copy_out, out_shape=tuple((jax.ShapeDtypeStruct(r.shape, r...  2 us

profile of v3, /device:TPU:256, one launch (start us, length us, event | category | flops | bytes accessed | tf_op | source)
XLA Modules:
  0.0 40.3 jit_solution(10144492395498727547)
XLA Ops:
  0.6 37.5 %shard_map.68 = (bf16[512,1024]{1,0:T(8,128)(2,1)}, f32[8,512]{1,0:T(8,128)}) custom-call(bf16[512,1024]{1,0:T(8,128)(2,1)} %q_hbm.1, bf16[64,1024]{1,0:T(8,128)(2,1)} %k_hbm.1, bf16[64,1024]{1,0:T(8,128)(2,1)} %v_hbm.1, s32[1,5]{1,0:T(1,128)} %mask_hbm.1, s32[1,512]{1,0:T(1,128)} %bitcast.1), custom_call_target="tpu_custom_call" | custom-call | tf_op jit(solution)/shard_map/pallas_call | solution.py:438
  38.2 2.0 %shard_map.69 = (bf16[512,1024]{1,0:T(8,128)(2,1)}, f32[8,512]{1,0:T(8,128)}) custom-call(bf16[512,1024]{1,0:T(8,128)(2,1)} %get-tuple-element.4.a_in, f32[8,512]{1,0:T(8,128)} %get-tuple-element.5.l_in), custom_call_target="tpu_custom_call" | custom-call | tf_op jit(solution)/shard_map/pallas_call | solution.py:467
